TPU v7x, 32 devices: a whole 2x2x4 slice. The times are simulated.
32 devices in a mesh: row: 4 (over y, core), col: 8 (over z, x).
Axes of the slice: x: 2, y: 2, z: 4, core: 2. Of those that a mesh axis runs over, the one named last changes fastest.
Arguments:
- rhs: bfloat16 [4, 4, 8, 64, 256], P(None, 'row', 'col'), may hold values from -6 to 6
- dinv: float32 [4, 4, 8, 64, 64], P(None, 'row', 'col'), may hold values from -1.5 to 1.5, as said below
- lower: bfloat16 [6, 4, 8, 8, 64, 128], P(None, 'row', 'col'), may hold values from -0.125 to 0.125
- sources: int32 [6, 4, 8, 8, 2], P(None, 'row', 'col'), may hold values from -1 to 3, as said below
Outputs:
- solution: float32 [4, 4, 8, 64, 256], P(None, 'row', 'col')
Inputs may be any that keep to these rules, and one draw needn't show every extreme that they name: `dinv`: lower triangular. `sources`: for each level pair, holder and target, the live entries are distinct; in every level pair every device has a target with all 2 entries live.
All inputs are finite; a program needn't handle non-finite values.
Results may differ from a plain program's by a relative error of at most 0.002.
Values may be sent and summed in bfloat16 or wider, within the bound.
A program may use at most 64 MiB of HBM per device.

v0:
```python
import jax
import jax.numpy as jnp
from jax import lax
from jax.sharding import PartitionSpec as P


def level_terms(blocks, indices, gathered):
    clipped = jnp.maximum(indices, 0)
    picked = jnp.take(gathered, clipped, axis=0)
    picked = jnp.where((indices >= 0)[:, :, None, None], picked, jnp.zeros((), gathered.dtype))
    peer_count, per_count, block_rows, rhs_width = picked.shape
    picked = picked.reshape(peer_count, per_count * block_rows, rhs_width)
    return jnp.einsum("qik,qkn->qin", blocks, picked, preferred_element_type=jnp.float32)


def on_device(rhs, dinv, lower, sources):
    levels = rhs.shape[0]
    block_rows = rhs.shape[3]
    rhs_width = rhs.shape[4]
    owned_acc = [jnp.zeros((block_rows, rhs_width), jnp.float32) for section in range(levels)]
    results = []
    pair_index = 0
    for section in range(levels):
        residual = rhs[section, 0, 0].astype(jnp.float32) - owned_acc[section]
        solution = jnp.dot(
            dinv[section, 0, 0],
            residual,
            precision=lax.Precision.HIGHEST,
            preferred_element_type=jnp.float32,
        )
        results.append(solution)
        if section + 1 < levels:
            solved = solution.astype(jnp.bfloat16)
            gathered = lax.all_gather(solved[None], "row", axis=0, tiled=True)
            partials = []
            for target in range(section + 1, levels):
                partials.append(
                    level_terms(lower[pair_index, 0, 0], sources[pair_index, 0, 0], gathered)
                )
                pair_index += 1
            arrived = lax.all_to_all(
                jnp.stack(partials, axis=1), "col", split_axis=0, concat_axis=0, tiled=True
            )
            summed = jnp.sum(arrived, axis=0)
            for position, target in enumerate(range(section + 1, levels)):
                owned_acc[target] = owned_acc[target] + summed[position]
    stacked = jnp.stack(results)
    return stacked[:, None, None]


def solution(mesh):
    in_specs = (
        P(None, "row", "col", None, None),
        P(None, "row", "col", None, None),
        P(None, "row", "col", None, None, None),
        P(None, "row", "col", None, None),
    )
    out_specs = P(None, "row", "col", None, None)
    return jax.shard_map(
        on_device, mesh=mesh, in_specs=in_specs, out_specs=out_specs, check_vma=False
    )
```

profile of v0, /device:TPU:0, one launch (start us, length us, event | category | flops | bytes accessed | tf_op | source)
XLA Modules:
  0.0 123.1 jit_solution(16928249831516090840)
XLA Ops:
  0.0 0.8 compare_and_fusion
  0.8 0.8 compare_bitcast_fusion
  1.7 0.9 fusion.46
  2.7 6.5 %all-gather = bf16[256,256]{1,0:T(8,128)(2,1)S(1)} all-gather(bf16[64,256]{1,0:T(8,128)(2,1)S(1)} %get-tuple-element.34), channel_id=2, replica_groups=mesh['row'=4,'col'=8] {'row'}, dimensions={0}, use_global_device_ids=true | all-gather | bytes 163840 | tf_op jit(solution)/shard_map/all_gather | solution.py:34
  9.5 0.6 gather_fusion.1
  10.1 0.6 gather_fusion
  11.1 0.2 convolution_bitcast_fusion.4
  11.4 0.2 convolution_bitcast_fusion.5
  11.8 0.6 gather_fusion.2
  13.1 1.3 %copy.52 = f32[8,3,64,256]{3,2,1,0:T(8,128)} copy(f32[8,3,64,256]{3,2,0,1:T(8,128)S(1)} %pad_maximum_fusion) | data formatting | bytes 3145728 | tf_op jit(solution)/shard_map/stack | solution.py:42
  14.4 6.2 %all-to-all-start = ((f32[8,3,64,256]{3,2,1,0:T(8,128)}), f32[8,3,64,256]{3,2,1,0:T(8,128)S(1)}, u32[]{:S(2)}, u32[]{:S(2)}) async-start(f32[8,3,64,256]{3,2,1,0:T(8,128)} %copy.52), calls=%async_computation | async-start | bytes 3145728 | tf_op jit(solution)/shard_map/all_to_all | solution.py:41
  21.4 36.8 %all-to-all-done = f32[8,3,64,256]{3,2,1,0:T(8,128)S(1)} async-done(((f32[8,3,64,256]{3,2,1,0:T(8,128)}), f32[8,3,64,256]{3,2,1,0:T(8,128)S(1)}, u32[]{:S(2)}, u32[]{:S(2)}) %all-to-all-start) | async-done | bytes 1572896 | tf_op jit(solution)/shard_map/all_to_all | solution.py:41
  58.5 5.4 %all-gather.1 = bf16[256,256]{1,0:T(8,128)(2,1)S(1)} all-gather(bf16[64,256]{1,0:T(8,128)(2,1)S(1)} %get-tuple-element.36), channel_id=3, replica_groups=mesh['row'=4,'col'=8] {'row'}, dimensions={0}, use_global_device_ids=true | all-gather | bytes 163840 | tf_op jit(solution)/shard_map/all_gather | solution.py:34
  63.9 0.6 gather_fusion.3
  64.6 0.2 convolution_bitcast_fusion.2
  64.9 0.6 gather_fusion.4
  65.6 0.2 convolution_bitcast_fusion.1
  65.9 1.1 copy.59
  67.0 3.6 %all-to-all-start.1 = ((f32[8,2,64,256]{3,2,1,0:T(8,128)}), f32[8,2,64,256]{3,2,1,0:T(8,128)S(1)}, u32[]{:S(2)}, u32[]{:S(2)}) async-start(f32[8,2,64,256]{3,2,1,0:T(8,128)} %copy.59), calls=%async_computation.1 | async-start | bytes 2097152 | tf_op jit(solution)/shard_map/all_to_all | solution.py:41
  71.0 26.0 %all-to-all-done.1 = f32[8,2,64,256]{3,2,1,0:T(8,128)S(1)} async-done(((f32[8,2,64,256]{3,2,1,0:T(8,128)}), f32[8,2,64,256]{3,2,1,0:T(8,128)S(1)}, u32[]{:S(2)}, u32[]{:S(2)}) %all-to-all-start.1) | async-done | bytes 1048608 | tf_op jit(solution)/shard_map/all_to_all | solution.py:41
  97.3 5.4 %all-gather.2 = bf16[256,256]{1,0:T(8,128)(2,1)S(1)} all-gather(bf16[64,256]{1,0:T(8,128)(2,1)S(1)} %get-tuple-element.38), channel_id=4, replica_groups=mesh['row'=4,'col'=8] {'row'}, dimensions={0}, use_global_device_ids=true | all-gather | bytes 163840 | tf_op jit(solution)/shard_map/all_gather | solution.py:34
  102.7 0.6 gather_fusion.5
  103.7 18.4 %all_to_all.15 = f32[8,1,64,256]{3,2,1,0:T(8,128)S(1)} all-to-all(f32[8,1,64,256]{3,2,1,0:T(8,128)S(1)} %convolution_bitcast_fusion), channel_id=1, replica_groups=mesh['row'=4,'col'=8] {'col'}, dimensions={0} | all-to-all | bytes 1048576 | tf_op jit(solution)/shard_map/all_to_all | solution.py:41
  122.3 0.7 maximum_bitcast_fusion
  (52 shorter events, 4.5 us)
Async XLA Ops:
  9.5 1.5 %copy-start = (bf16[6,1,1,8,64,128]{5,4,3,2,1,0:T(8,128)(2,1)S(1)}, bf16[6,1,1,8,64,128]{5,4,3,2,1,0:T(8,128)(2,1)}, u32[]{:S(2)}) copy-start(bf16[6,1,1,8,64,128]{5,4,3,2,1,0:T(8,128)(2,1)} %param.8) | copy-start | bytes 2359300
  14.4 43.7 %all-to-all-start = ((f32[8,3,64,256]{3,2,1,0:T(8,128)}), f32[8,3,64,256]{3,2,1,0:T(8,128)S(1)}, u32[]{:S(2)}, u32[]{:S(2)}) async-start(f32[8,3,64,256]{3,2,1,0:T(8,128)} %copy.52), calls=%async_computation | async-start | bytes 3145728 | tf_op jit(solution)/shard_map/all_to_all | solution.py:41
  20.6 37.6 %copy-start.1 = (f32[4,1,1,64,64]{4,3,2,1,0:T(8,128)S(1)}, f32[4,1,1,64,64]{4,3,2,1,0:T(8,128)}, u32[]{:S(2)}) copy-start(f32[4,1,1,64,64]{4,3,2,1,0:T(8,128)} %param.7) | copy-start | bytes 196612
  20.6 37.6 %copy-start.2 = (bf16[4,1,1,64,256]{4,3,2,1,0:T(8,128)(2,1)S(1)}, bf16[4,1,1,64,256]{4,3,2,1,0:T(8,128)(2,1)}, u32[]{:S(2)}) copy-start(bf16[4,1,1,64,256]{4,3,2,1,0:T(8,128)(2,1)} %param.6) | copy-start | bytes 393220
  67.0 30.0 %all-to-all-start.1 = ((f32[8,2,64,256]{3,2,1,0:T(8,128)}), f32[8,2,64,256]{3,2,1,0:T(8,128)S(1)}, u32[]{:S(2)}, u32[]{:S(2)}) async-start(f32[8,2,64,256]{3,2,1,0:T(8,128)} %copy.59), calls=%async_computation.1 | async-start | bytes 2097152 | tf_op jit(solution)/shard_map/all_to_all | solution.py:41
where the time goes:
time: 123 us
  waiting for transfers between devices  62.8 us (51%)
  blocking collectives  35.8 us (29%)
  starting transfers between devices  9.8 us (8%)
  local copies, waits for them, and re-layouts  7.98 us (6%)
  other arithmetic  3.61 us (3%)
  matrix products  2.84 us (2%)
    all_to_all x2, waiting for transfers between devices, on_device(): lax.all_to_all(jnp.stack(partials, axis=1), 'col', split_axis=0, concat_a...  62.8 us
    all_to_all x1, blocking collectives, on_device(): lax.all_to_all(jnp.stack(partials, axis=1), 'col', split_axis=0, concat_a...  18.4 us
    all_gather x3, blocking collectives, on_device(): gathered = lax.all_gather(solved[None], 'row', axis=0, tiled=True)  17.4 us
    all_to_all x2, starting transfers between devices, on_device(): lax.all_to_all(jnp.stack(partials, axis=1), 'col', split_axis=0, concat_a...  9.8 us
    gather x6, local copies, waits for them, and re-layouts, level_terms(): picked = jnp.take(gathered, clipped, axis=0)  3.48 us
  transfers between devices with their start and end apart: 2, of which 2 were waited for; matrix products, arithmetic and copies ran while one was open for 1% of the time, Pallas kernels for 0%

commit v1 on v0

v1 whole, which is shorter than its diff:
```python
import functools

import jax
import jax.numpy as jnp
from jax import lax
from jax.experimental import pallas as pl
from jax.experimental.pallas import tpu as pltpu
from jax.sharding import PartitionSpec as P

MESH = pl.DeviceIdType.MESH
BF16 = jnp.bfloat16
F32 = jnp.float32


def pair_of(levels, solved, target):
    return sum(levels - 1 - l for l in range(solved)) + target - solved - 1


def kernel(
    rows, groups, pair, parts,
    rhs, dinv, lower, sources, out,
    wide, held, gathered, outgoing, arrived, summed, far_sources, own_s, far_s,
    gsend, grecv, ssend, srecv, lsend, lrecv, csend, crecv, local_sem,
):
    levels, bs, width = rhs.shape
    part = width // parts
    last = levels - 1
    row = lax.axis_index("row")
    col = lax.axis_index("col")
    group = col // pair
    side = col % pair

    near = [(kr, kb) for kb in reversed(range(pair)) for kr in reversed(range(rows)) if (kr, kb) != (0, 0)]
    far = list(reversed(range(1, groups)))

    def near_device(kr, kb):
        return ((row + kr) % rows, group * pair + (side + kb) % pair)

    def far_device(ka):
        return (row, ((group + ka) % groups) * pair + side)

    barrier = pltpu.get_barrier_semaphore()
    for kr, kb in near:
        pl.semaphore_signal(barrier, inc=1, device_id=near_device(kr, kb), device_id_type=MESH)
    for ka in far:
        pl.semaphore_signal(barrier, inc=1, device_id=far_device(ka), device_id_type=MESH)

    def cols(h):
        return pl.ds(h * part, part)

    def solve(l, h):
        residual = rhs[l, :, cols(h)].astype(F32)
        if l > 0:
            acc = summed[h, group]
            for i in range(groups - 1):
                acc = acc + arrived[l - 1, h, i].astype(F32)
            residual = residual - acc
        solution = jnp.dot(
            dinv[l], residual, precision=lax.Precision.HIGHEST, preferred_element_type=F32
        )
        out[l, :, cols(h)] = solution
        if l < last:
            gathered[l, h, side, row] = solution.astype(BF16)

    def gather_copies(l, h):
        block = gathered.at[l, h, side, row]
        return [
            pltpu.make_async_remote_copy(
                src_ref=block, dst_ref=block,
                send_sem=gsend.at[l, h, i], recv_sem=grecv.at[l, h, i],
                device_id=near_device(kr, kb), device_id_type=MESH,
            )
            for i, (kr, kb) in enumerate(near)
        ]

    def scatter_copies(l, h):
        return [
            pltpu.make_async_remote_copy(
                src_ref=outgoing.at[l, h, (group + ka) % groups], dst_ref=arrived.at[l, h, i],
                send_sem=ssend.at[l, h, i], recv_sem=srecv.at[l, h, i],
                device_id=far_device(ka), device_id_type=MESH,
            )
            for i, ka in enumerate(far)
        ]

    def lower_copies(target):
        found = []
        for l in range(target):
            p = pair_of(levels, l, target)
            for kb in range(1, pair):
                found.append((p, pltpu.make_async_remote_copy(
                    src_ref=lower.at[p, :, (side + kb) % pair], dst_ref=held.at[p, kb - 1],
                    send_sem=lsend.at[p, kb - 1], recv_sem=lrecv.at[p, kb - 1],
                    device_id=near_device(0, kb), device_id_type=MESH,
                )))
        return found

    def source_copies():
        return [
            pltpu.make_async_remote_copy(
                src_ref=sources, dst_ref=far_sources.at[kb - 1],
                send_sem=csend.at[kb - 1], recv_sem=crecv.at[kb - 1],
                device_id=near_device(0, kb), device_id_type=MESH,
            )
            for kb in range(1, pair)
        ]

    lane = lax.broadcasted_iota(jnp.int32, (bs, 2 * bs), 1)
    first = lane < bs

    def spread(p, index_of, block_of, from_side):
        def one(g, carry):
            base = (g * pair + side) * 2
            s0 = index_of(base)
            s1 = index_of(base + 1)
            block = block_of(g)
            in_place = jnp.where(first, s0, s1)
            across = jnp.where(first, s1, s0)
            swapped = jnp.concatenate([block[:, bs:], block[:, :bs]], axis=1)
            for two in range(rows // 2):
                even, odd = 2 * two, 2 * two + 1
                wanted = jnp.where(first, even, odd)
                straight = jnp.where(in_place == wanted, 1.0, 0.0).astype(BF16)
                crossed = jnp.where(across == wanted, 1.0, 0.0).astype(BF16)
                wide[p, from_side, g, :, 2 * two * bs:(2 * two + 2) * bs] = (
                    block * straight + swapped * crossed
                )
            return carry

        if groups <= 4:
            for g in range(groups):
                one(g, 0)
        else:
            lax.fori_loop(0, groups, one, 0)

    def spread_own(target):
        for l in range(target):
            p = pair_of(levels, l, target)
            spread(p, lambda i, p=p: own_s[p, i], lambda g, p=p: lower[p, g, side], side)

    def spread_far(target):
        for p, copy in lower_copies(target):
            copy.wait_recv()
        for l in range(target):
            p = pair_of(levels, l, target)
            for kb in range(1, pair):
                spread(
                    p, lambda i, p=p, kb=kb: far_s[kb - 1, p, i],
                    lambda g, p=p, kb=kb: held[p, kb - 1, g],
                    (side + pair - kb) % pair,
                )

    chunk = min(groups, 4)

    def product(l, target, h, begin):
        p = pair_of(levels, l, target)
        total = None
        for s in range(pair):
            left = wide[p, s, pl.ds(begin, chunk)].reshape(chunk * bs, rows * bs)
            right = gathered[l, h, s].reshape(rows * bs, part)
            term = jnp.dot(left, right, preferred_element_type=F32)
            total = term if total is None else total + term
        return total.reshape(chunk, bs, part)

    def over_chunks(body):
        if groups == chunk:
            body(0)
        else:
            def step(i, carry):
                body(i * chunk)
                return carry
            lax.fori_loop(0, groups // chunk, step, 0)

    def earlier_terms(l, h):
        def body(begin):
            total = product(0, l + 1, h, begin)
            for m in range(1, l):
                total = total + product(m, l + 1, h, begin)
            summed[h, pl.ds(begin, chunk)] = total
        if l > 0:
            over_chunks(body)

    def newest_term(l, h):
        def body(begin):
            total = product(l, l + 1, h, begin)
            if l > 0:
                total = total + summed[h, pl.ds(begin, chunk)]
            summed[h, pl.ds(begin, chunk)] = total
            outgoing[l, h, pl.ds(begin, chunk)] = total.astype(BF16)
        over_chunks(body)

    own_copy = pltpu.make_async_copy(sources, own_s, local_sem.at[0])
    own_copy.start()
    for h in range(parts):
        solve(0, h)
    own_copy.wait()
    spread_own(1)
    pl.semaphore_wait(barrier, len(near) + len(far))
    for copy in source_copies():
        copy.start()

    for l in range(last):
        for h in range(parts):
            if l > 0:
                for copy in scatter_copies(l - 1, h):
                    copy.wait_recv()
                solve(l, h)
            for copy in gather_copies(l, h):
                copy.start()
            if l == 0 and h == 0:
                for p, copy in lower_copies(1):
                    copy.start()
        if l == 0:
            for i, copy in enumerate(source_copies()):
                copy.wait_recv()
                back = pltpu.make_async_copy(far_sources.at[i], far_s.at[i], local_sem.at[1 + i])
                back.start()
                back.wait()
        spread_far(l + 1)
        for h in range(parts):
            earlier_terms(l, h)
        for h in range(parts):
            for copy in gather_copies(l, h):
                copy.wait_recv()
            newest_term(l, h)
            for copy in scatter_copies(l, h):
                copy.start()
        if l + 1 < last:
            for p, copy in lower_copies(l + 2):
                copy.start()
            spread_own(l + 2)
    for h in range(parts):
        for copy in scatter_copies(last - 1, h):
            copy.wait_recv()
        solve(last, h)

    for copy in source_copies():
        copy.wait_send()
    for l in range(last):
        for p, copy in lower_copies(l + 1):
            copy.wait_send()
        for h in range(parts):
            for copy in gather_copies(l, h) + scatter_copies(l, h):
                copy.wait_send()


def on_device(rows, columns, rhs, dinv, lower, sources):
    levels, _, _, bs, width = rhs.shape
    pairs = lower.shape[0]
    per = sources.shape[-1]
    pair = 2
    parts = 2
    groups = columns // pair
    part = width // parts
    last = levels - 1
    near = rows * pair - 1
    far = groups - 1
    dma = pltpu.SemaphoreType.DMA
    flops = 2 * pairs * groups * bs * pair * rows * bs * width
    result = pl.pallas_call(
        functools.partial(kernel, rows, groups, pair, parts),
        out_shape=jax.ShapeDtypeStruct((levels, bs, width), F32),
        in_specs=[pl.BlockSpec(memory_space=pltpu.VMEM)] * 4,
        out_specs=pl.BlockSpec(memory_space=pltpu.VMEM),
        scratch_shapes=[
            pltpu.VMEM((pairs, pair, groups, bs, rows * bs), BF16),
            pltpu.VMEM((pairs, pair - 1, groups, bs, per * bs), BF16),
            pltpu.VMEM((last, parts, pair, rows, bs, part), BF16),
            pltpu.VMEM((last, parts, groups, bs, part), BF16),
            pltpu.VMEM((last, parts, far, bs, part), BF16),
            pltpu.VMEM((parts, groups, bs, part), F32),
            pltpu.VMEM((pair - 1, pairs, columns * per), jnp.int32),
            pltpu.SMEM((pairs, columns * per), jnp.int32),
            pltpu.SMEM((pair - 1, pairs, columns * per), jnp.int32),
            dma((last, parts, near)),
            dma((last, parts, near)),
            dma((last, parts, far)),
            dma((last, parts, far)),
            dma((pairs, pair - 1)),
            dma((pairs, pair - 1)),
            dma((pair - 1,)),
            dma((pair - 1,)),
            dma((pair,)),
        ],
        compiler_params=pltpu.CompilerParams(
            collective_id=0, has_side_effects=True, vmem_limit_bytes=48 * 1024 * 1024
        ),
        cost_estimate=pl.CostEstimate(
            flops=flops, bytes_accessed=2 * lower.size, transcendentals=0
        ),
    )(
        rhs.reshape(levels, bs, width),
        dinv.reshape(levels, bs, bs),
        lower.reshape(pairs, groups, pair, bs, per * bs),
        sources.reshape(pairs, columns * per),
    )
    return result.reshape(levels, 1, 1, bs, width)


def solution(mesh):
    in_specs = (
        P(None, "row", "col", None, None),
        P(None, "row", "col", None, None),
        P(None, "row", "col", None, None, None),
        P(None, "row", "col", None, None),
    )
    out_specs = P(None, "row", "col", None, None)
    return jax.shard_map(
        functools.partial(on_device, mesh.shape["row"], mesh.shape["col"]),
        mesh=mesh, in_specs=in_specs, out_specs=out_specs, check_vma=False,
    )
```

time: 123 us -> 39.1 us (0.32)
  waiting for transfers between devices: 62.8 us -> 0 us
  blocking collectives: 35.8 us -> 0 us
  Pallas kernels: 0 us -> 34.3 us
  starting transfers between devices: 9.8 us -> 0 us
  other arithmetic: 3.61 us -> 0 us
  local copies, waits for them, and re-layouts: 7.98 us -> 4.51 us
  matrix products: 2.84 us -> 0 us
    all_to_all x2 -> x0, waiting for transfers between devices: 62.8 us -> none  [on_device(): lax.all_to_all(jnp.stack(partials, axis=1), 'col', split_axis=0, concat_a...]
    pallas_call x0 -> x1, Pallas kernels: none -> 34.3 us  [on_device(): pl.pallas_call(functools.partial(kernel, rows, groups, pair, parts), out_...]
    all_to_all x1 -> x0, blocking collectives: 18.4 us -> none  [on_device(): lax.all_to_all(jnp.stack(partials, axis=1), 'col', split_axis=0, concat_a...]
    all_gather x3 -> x0, blocking collectives: 17.4 us -> none  [on_device(): gathered = lax.all_gather(solved[None], 'row', axis=0, tiled=True)]
    all_to_all x2 -> x0, starting transfers between devices: 9.8 us -> none  [on_device(): lax.all_to_all(jnp.stack(partials, axis=1), 'col', split_axis=0, concat_a...]
    unnamed x6 -> x8, local copies, waits for them, and re-layouts: 0.01 us -> 4.42 us
    gather x6 -> x0, local copies, waits for them, and re-layouts: 3.48 us -> none  [level_terms(): picked = jnp.take(gathered, clipped, axis=0)]
    dot_general x10 -> x0, matrix products: 2.84 us -> none  [the longest x4 1.55 us: on_device(): jnp.dot(dinv[section, 0, 0], residual, precision=lax.Precision.HIGHEST, p...]
  transfers between devices with their start and end apart: 2 -> 0, of which waited for: 2 -> 0; matrix products, arithmetic and copies ran while one was open for 1% -> 0% of each run, Pallas kernels for 0% -> 0%
where the time goes in v1:
time: 39.1 us; the launch traced here: 38.8 us
  Pallas kernels  34.3 us (88%)
  local copies, waits for them, and re-layouts  4.51 us (12%)
    pallas_call x1, Pallas kernels, on_device(): pl.pallas_call(functools.partial(kernel, rows, groups, pair, parts), out_...  34.3 us
    unnamed x8, local copies, waits for them, and re-layouts  4.42 us

profile of v1, /device:TPU:0, one launch (start us, length us, event | category | flops | bytes accessed | tf_op | source)
XLA Modules:
  0.0 38.8 jit_solution(6251542646475776567)
XLA Ops:
  0.0 0.8 %copy.5 = s32[6,1,1,8,2]{0,4,3,2,1:T(2,128)S(1)} copy(s32[6,1,1,8,2]{3,4,2,1,0:T(2,128)} %param.7) | data formatting | bytes 768 | tf_op args[3]
  0.8 0.1 copy.6.sources
  0.9 0.0 copy-start
  0.9 1.1 %copy-done = bf16[6,1,1,8,64,128]{5,4,3,2,1,0:T(8,128)(2,1)S(1)} copy-done((bf16[6,1,1,8,64,128]{5,4,3,2,1,0:T(8,128)(2,1)S(1)}, bf16[6,1,1,8,64,128]{5,4,3,2,1,0:T(8,128)(2,1)}, u32[]{:S(2)}) %copy-start) | copy-done | bytes 786456
  2.0 0.0 copy-start.1
  2.0 0.9 %copy-done.1 = bf16[4,1,1,64,256]{4,3,2,1,0:T(8,128)(2,1)S(1)} copy-done((bf16[4,1,1,64,256]{4,3,2,1,0:T(8,128)(2,1)S(1)}, bf16[4,1,1,64,256]{4,3,2,1,0:T(8,128)(2,1)}, u32[]{:S(2)}) %copy-start.1) | copy-done | bytes 131096
  2.9 0.0 copy-start.2
  2.9 0.9 %copy-done.2 = f32[4,1,1,64,64]{4,3,2,1,0:T(8,128)S(1)} copy-done((f32[4,1,1,64,64]{4,3,2,1,0:T(8,128)S(1)}, f32[4,1,1,64,64]{4,3,2,1,0:T(8,128)}, u32[]{:S(2)}) %copy-start.2) | copy-done | bytes 65560
  3.8 34.3 %shard_map.46 = f32[4,64,256]{2,1,0:T(8,128)S(1)} custom-call(bf16[4,64,256]{2,1,0:T(8,128)(2,1)S(1)} %bitcast.9, f32[4,64,64]{2,1,0:T(8,128)S(1)} %bitcast.10, bf16[6,4,2,64,128]{4,3,2,1,0:T(8,128)(2,1)S(1)} %bitcast.8, s32[6,16]{1,0:T(8,128)S(1)} %copy.6.sources), custom_call_target="tpu_custom_call" | custom-call | flops 402653184 | bytes 786432 | tf_op jit(solution)/shard_map/pallas_call | solution.py:260
  38.1 0.7 %copy.9 = f32[4,1,1,64,256]{4,3,2,1,0:T(8,128)} copy(f32[4,1,1,64,256]{4,3,2,1,0:T(8,128)S(1)} %bitcast.7) | data formatting | bytes 524288
Async XLA Ops:
  0.9 1.1 %copy-start = (bf16[6,1,1,8,64,128]{5,4,3,2,1,0:T(8,128)(2,1)S(1)}, bf16[6,1,1,8,64,128]{5,4,3,2,1,0:T(8,128)(2,1)}, u32[]{:S(2)}) copy-start(bf16[6,1,1,8,64,128]{5,4,3,2,1,0:T(8,128)(2,1)} %param.6) | copy-start | bytes 2359300
  2.0 0.9 %copy-start.1 = (bf16[4,1,1,64,256]{4,3,2,1,0:T(8,128)(2,1)S(1)}, bf16[4,1,1,64,256]{4,3,2,1,0:T(8,128)(2,1)}, u32[]{:S(2)}) copy-start(bf16[4,1,1,64,256]{4,3,2,1,0:T(8,128)(2,1)} %param.4) | copy-start | bytes 393220
  2.9 0.9 %copy-start.2 = (f32[4,1,1,64,64]{4,3,2,1,0:T(8,128)S(1)}, f32[4,1,1,64,64]{4,3,2,1,0:T(8,128)}, u32[]{:S(2)}) copy-start(f32[4,1,1,64,64]{4,3,2,1,0:T(8,128)} %param.5) | copy-start | bytes 196612

commit v2 on v1

--- a/solution.py
+++ b/solution.py
@@ -18,9 +18,10 @@
 
 def kernel(
     rows, groups, pair, parts,
-    rhs, dinv, lower, sources, out,
-    wide, held, gathered, outgoing, arrived, summed, far_sources, own_s, far_s,
-    gsend, grecv, ssend, srecv, lsend, lrecv, csend, crecv, local_sem,
+    rhs_hbm, dinv_hbm, lower, sources, out_hbm,
+    out, rhs, dinv, split, mine, wide, held, gathered, outgoing, arrived, summed,
+    far_sources, own_s, far_s,
+    gsend, grecv, ssend, srecv, lsend, lrecv, csend, crecv, local_sem, out_sem,
 ):
     levels, bs, width = rhs.shape
     part = width // parts
@@ -29,6 +30,17 @@
     col = lax.axis_index("col")
     group = col // pair
     side = col % pair
+    blocks = pair * rows
+
+    loads = [
+        pltpu.make_async_copy(rhs_hbm, rhs, local_sem.at[0]),
+        pltpu.make_async_copy(dinv_hbm, dinv, local_sem.at[1]),
+        pltpu.make_async_copy(sources, own_s, local_sem.at[2]),
+        pltpu.make_async_copy(lower.at[0, :, side], mine.at[0], local_sem.at[3]),
+        pltpu.make_async_copy(lower.at[1:, :, side], mine.at[1:], local_sem.at[4]),
+    ]
+    for load in loads:
+        load.start()
 
     near = [(kr, kb) for kb in reversed(range(pair)) for kr in reversed(range(rows)) if (kr, kb) != (0, 0)]
     far = list(reversed(range(1, groups)))
@@ -47,6 +59,11 @@
 
     def cols(h):
         return pl.ds(h * part, part)
+
+    def result_copy(l, h):
+        return pltpu.make_async_copy(
+            out.at[l, :, cols(h)], out_hbm.at[l, :, cols(h)], out_sem.at[l, h]
+        )
 
     def solve(l, h):
         residual = rhs[l, :, cols(h)].astype(F32)
@@ -55,33 +72,55 @@
             for i in range(groups - 1):
                 acc = acc + arrived[l - 1, h, i].astype(F32)
             residual = residual - acc
+        high = residual.astype(BF16)
+        low = (residual - high.astype(F32)).astype(BF16)
         solution = jnp.dot(
-            dinv[l], residual, precision=lax.Precision.HIGHEST, preferred_element_type=F32
+            split[l], jnp.concatenate([high, low, high, low], axis=0),
+            preferred_element_type=F32,
         )
         out[l, :, cols(h)] = solution
         if l < last:
-            gathered[l, h, side, row] = solution.astype(BF16)
+            gathered[l, h, side * rows + row] = solution.astype(BF16)
+        result_copy(l, h).start()
 
     def gather_copies(l, h):
-        block = gathered.at[l, h, side, row]
+        block = gathered.at[l, h, side * rows + row]
         return [
             pltpu.make_async_remote_copy(
                 src_ref=block, dst_ref=block,
-                send_sem=gsend.at[l, h, i], recv_sem=grecv.at[l, h, i],
+                send_sem=gsend.at[l], recv_sem=grecv.at[l, h],
                 device_id=near_device(kr, kb), device_id_type=MESH,
             )
-            for i, (kr, kb) in enumerate(near)
+            for kr, kb in near
         ]
 
     def scatter_copies(l, h):
         return [
             pltpu.make_async_remote_copy(
                 src_ref=outgoing.at[l, h, (group + ka) % groups], dst_ref=arrived.at[l, h, i],
-                send_sem=ssend.at[l, h, i], recv_sem=srecv.at[l, h, i],
+                send_sem=ssend.at[l], recv_sem=srecv.at[l, h],
                 device_id=far_device(ka), device_id_type=MESH,
             )
             for i, ka in enumerate(far)
         ]
+
+    def bytes_of(ref, send_sem, recv_sem, device):
+        return pltpu.make_async_remote_copy(
+            src_ref=ref, dst_ref=ref, send_sem=send_sem, recv_sem=recv_sem,
+            device_id=device, device_id_type=MESH,
+        )
+
+    def wait_gather(l, h):
+        ref = gathered.at[l, h, pl.ds(0, blocks - 1)]
+        bytes_of(ref, gsend.at[l], grecv.at[l, h], near_device(*near[0])).wait_recv()
+
+    def wait_scatter(l, h):
+        bytes_of(arrived.at[l, h], ssend.at[l], srecv.at[l, h], far_device(far[0])).wait_recv()
+
+    def wait_sends(l):
+        ref = gathered.at[l, :, pl.ds(0, blocks - 1)]
+        bytes_of(ref, gsend.at[l], grecv.at[l, 0], near_device(*near[0])).wait_send()
+        bytes_of(arrived.at[l], ssend.at[l], srecv.at[l, 0], far_device(far[0])).wait_send()
 
     def lower_copies(target):
         found = []
@@ -110,9 +149,8 @@
 
     def spread(p, index_of, block_of, from_side):
         def one(g, carry):
-            base = (g * pair + side) * 2
-            s0 = index_of(base)
-            s1 = index_of(base + 1)
+            s0 = index_of(0, g * pair + side)
+            s1 = index_of(1, g * pair + side)
             block = block_of(g)
             in_place = jnp.where(first, s0, s1)
             across = jnp.where(first, s1, s0)
@@ -136,7 +174,7 @@
     def spread_own(target):
         for l in range(target):
             p = pair_of(levels, l, target)
-            spread(p, lambda i, p=p: own_s[p, i], lambda g, p=p: lower[p, g, side], side)
+            spread(p, lambda e, q, p=p: own_s[p, e, q], lambda g, p=p: mine[p, g], side)
 
     def spread_far(target):
         for p, copy in lower_copies(target):
@@ -145,7 +183,7 @@
             p = pair_of(levels, l, target)
             for kb in range(1, pair):
                 spread(
-                    p, lambda i, p=p, kb=kb: far_s[kb - 1, p, i],
+                    p, lambda e, q, p=p, kb=kb: far_s[kb - 1, p, e, q],
                     lambda g, p=p, kb=kb: held[p, kb - 1, g],
                     (side + pair - kb) % pair,
                 )
@@ -157,7 +195,7 @@
         total = None
         for s in range(pair):
             left = wide[p, s, pl.ds(begin, chunk)].reshape(chunk * bs, rows * bs)
-            right = gathered[l, h, s].reshape(rows * bs, part)
+            right = gathered[l, h, s * rows:(s + 1) * rows].reshape(rows * bs, part)
             term = jnp.dot(left, right, preferred_element_type=F32)
             total = term if total is None else total + term
         return total.reshape(chunk, bs, part)
@@ -189,11 +227,16 @@
             outgoing[l, h, pl.ds(begin, chunk)] = total.astype(BF16)
         over_chunks(body)
 
-    own_copy = pltpu.make_async_copy(sources, own_s, local_sem.at[0])
-    own_copy.start()
+    loads[0].wait()
+    loads[1].wait()
+    for l in range(levels):
+        high = dinv[l].astype(BF16)
+        low = (dinv[l] - high.astype(F32)).astype(BF16)
+        split[l] = jnp.concatenate([high, high, low, low], axis=1)
     for h in range(parts):
         solve(0, h)
-    own_copy.wait()
+    loads[2].wait()
+    loads[3].wait()
     spread_own(1)
     pl.semaphore_wait(barrier, len(near) + len(far))
     for copy in source_copies():
@@ -202,8 +245,7 @@
     for l in range(last):
         for h in range(parts):
             if l > 0:
-                for copy in scatter_copies(l - 1, h):
-                    copy.wait_recv()
+                wait_scatter(l - 1, h)
                 solve(l, h)
             for copy in gather_copies(l, h):
                 copy.start()
@@ -213,35 +255,40 @@
         if l == 0:
             for i, copy in enumerate(source_copies()):
                 copy.wait_recv()
-                back = pltpu.make_async_copy(far_sources.at[i], far_s.at[i], local_sem.at[1 + i])
+                back = pltpu.make_async_copy(far_sources.at[i], far_s.at[i], local_sem.at[5 + i])
                 back.start()
                 back.wait()
         spread_far(l + 1)
         for h in range(parts):
             earlier_terms(l, h)
         for h in range(parts):
-            for copy in gather_copies(l, h):
-                copy.wait_recv()
+            wait_gather(l, h)
             newest_term(l, h)
             for copy in scatter_copies(l, h):
                 copy.start()
         if l + 1 < last:
             for p, copy in lower_copies(l + 2):
                 copy.start()
+            if l == 0:
+                loads[4].wait()
             spread_own(l + 2)
-    for h in range(parts):
-        for copy in scatter_copies(last - 1, h):
-            copy.wait_recv()
-        solve(last, h)
-
+            for p, copy in lower_copies(l + 1):
+                copy.wait_send()
+            if l > 0:
+                wait_sends(l - 1)
     for copy in source_copies():
         copy.wait_send()
-    for l in range(last):
-        for p, copy in lower_copies(l + 1):
-            copy.wait_send()
+    for p, copy in lower_copies(last):
+        copy.wait_send()
+    for l in range(max(last - 2, 0), last - 1):
+        wait_sends(l)
+    for h in range(parts):
+        wait_scatter(last - 1, h)
+        solve(last, h)
+    wait_sends(last - 1)
+    for l in range(levels):
         for h in range(parts):
-            for copy in gather_copies(l, h) + scatter_copies(l, h):
-                copy.wait_send()
+            result_copy(l, h).wait()
 
 
 def on_device(rows, columns, rhs, dinv, lower, sources):
@@ -253,37 +300,42 @@
     groups = columns // pair
     part = width // parts
     last = levels - 1
-    near = rows * pair - 1
     far = groups - 1
     dma = pltpu.SemaphoreType.DMA
     flops = 2 * pairs * groups * bs * pair * rows * bs * width
     result = pl.pallas_call(
         functools.partial(kernel, rows, groups, pair, parts),
         out_shape=jax.ShapeDtypeStruct((levels, bs, width), F32),
-        in_specs=[pl.BlockSpec(memory_space=pltpu.VMEM)] * 4,
-        out_specs=pl.BlockSpec(memory_space=pltpu.VMEM),
+        in_specs=[pl.BlockSpec(memory_space=pltpu.HBM)] * 4,
+        out_specs=pl.BlockSpec(memory_space=pltpu.HBM),
         scratch_shapes=[
+            pltpu.VMEM((levels, bs, width), F32),
+            pltpu.VMEM((levels, bs, width), BF16),
+            pltpu.VMEM((levels, bs, bs), F32),
+            pltpu.VMEM((levels, bs, 4 * bs), BF16),
+            pltpu.VMEM((pairs, groups, bs, per * bs), BF16),
             pltpu.VMEM((pairs, pair, groups, bs, rows * bs), BF16),
             pltpu.VMEM((pairs, pair - 1, groups, bs, per * bs), BF16),
-            pltpu.VMEM((last, parts, pair, rows, bs, part), BF16),
+            pltpu.VMEM((last, parts, pair * rows, bs, part), BF16),
             pltpu.VMEM((last, parts, groups, bs, part), BF16),
             pltpu.VMEM((last, parts, far, bs, part), BF16),
             pltpu.VMEM((parts, groups, bs, part), F32),
-            pltpu.VMEM((pair - 1, pairs, columns * per), jnp.int32),
-            pltpu.SMEM((pairs, columns * per), jnp.int32),
-            pltpu.SMEM((pair - 1, pairs, columns * per), jnp.int32),
-            dma((last, parts, near)),
-            dma((last, parts, near)),
-            dma((last, parts, far)),
-            dma((last, parts, far)),
+            pltpu.VMEM((pair - 1, pairs, per, columns), jnp.int32),
+            pltpu.SMEM((pairs, per, columns), jnp.int32),
+            pltpu.SMEM((pair - 1, pairs, per, columns), jnp.int32),
+            dma((last,)),
+            dma((last, parts)),
+            dma((last,)),
+            dma((last, parts)),
             dma((pairs, pair - 1)),
             dma((pairs, pair - 1)),
             dma((pair - 1,)),
             dma((pair - 1,)),
-            dma((pair,)),
+            dma((4 + pair,)),
+            dma((levels, parts)),
         ],
         compiler_params=pltpu.CompilerParams(
-            collective_id=0, has_side_effects=True, vmem_limit_bytes=48 * 1024 * 1024
+            collective_id=0, has_side_effects=True, vmem_limit_bytes=64 * 1024 * 1024
         ),
         cost_estimate=pl.CostEstimate(
             flops=flops, bytes_accessed=2 * lower.size, transcendentals=0
@@ -292,7 +344,7 @@
         rhs.reshape(levels, bs, width),
         dinv.reshape(levels, bs, bs),
         lower.reshape(pairs, groups, pair, bs, per * bs),
-        sources.reshape(pairs, columns * per),
+        jnp.swapaxes(sources.reshape(pairs, columns, per), 1, 2),
     )
     return result.reshape(levels, 1, 1, bs, width)
 

time: 39.1 us -> 36.3 us (0.928)
  local copies, waits for them, and re-layouts: 4.51 us -> 1.67 us
    unnamed x8 -> x1, local copies, waits for them, and re-layouts: 4.42 us -> 1.67 us
where the time goes in v2:
time: 36.3 us; the launch traced here: 36.2 us
  Pallas kernels  34.5 us (95%)
  local copies, waits for them, and re-layouts  1.67 us (5%)
    pallas_call x1, Pallas kernels, on_device(): pl.pallas_call(functools.partial(kernel, rows, groups, pair, parts), out_...  34.5 us
    unnamed x1, local copies, waits for them, and re-layouts  1.67 us

profile of v2, /device:TPU:0, one launch (start us, length us, event | category | flops | bytes accessed | tf_op | source)
XLA Modules:
  0.0 36.2 jit_solution(9747495447291722857)
XLA Ops:
  0.0 34.5 %shard_map.46 = f32[4,64,256]{2,1,0:T(8,128)} custom-call(bf16[4,64,256]{2,1,0:T(8,128)(2,1)} %bitcast.11, f32[4,64,64]{2,1,0:T(8,128)} %bitcast.12, bf16[6,4,2,64,128]{4,3,2,1,0:T(8,128)(2,1)} %bitcast.10, s32[6,2,8]{2,1,0:T(2,128)} %bitcast.13), custom_call_target="tpu_custom_call" | custom-call | flops 402653184 | bytes 786432 | tf_op jit(solution)/shard_map/pallas_call | solution.py:306
  34.5 1.7 %copy.7 = f32[4,1,1,64,256]{4,3,2,1,0:T(8,128)} copy(f32[4,1,1,64,256]{4,3,2,1,0:T(8,128)} %bitcast.9) | data formatting | bytes 524288

commit v3 on v2

--- a/solution.py
+++ b/solution.py
@@ -18,10 +18,10 @@
 
 def kernel(
     rows, groups, pair, parts,
-    rhs_hbm, dinv_hbm, lower, sources, out_hbm,
-    out, rhs, dinv, split, mine, wide, held, gathered, outgoing, arrived, summed,
+    rhs_hbm, dinv_hbm, lower, sources, out,
+    rhs, dinv, split, mine, wide, held, gathered, outgoing, arrived, summed,
     far_sources, own_s, far_s,
-    gsend, grecv, ssend, srecv, lsend, lrecv, csend, crecv, local_sem, out_sem,
+    gsend, grecv, ssend, srecv, lsend, lrecv, csend, crecv, local_sem, trecv,
 ):
     levels, bs, width = rhs.shape
     part = width // parts
@@ -42,7 +42,8 @@
     for load in loads:
         load.start()
 
-    near = [(kr, kb) for kb in reversed(range(pair)) for kr in reversed(range(rows)) if (kr, kb) != (0, 0)]
+    near = [(kr, kb) for kb in reversed(range(pair)) for kr in reversed(range(0, rows, 2)) if (kr, kb) != (0, 0)]
+    twin = (row + 1 - 2 * (row % 2), col)
     far = list(reversed(range(1, groups)))
 
     def near_device(kr, kb):
@@ -54,21 +55,17 @@
     barrier = pltpu.get_barrier_semaphore()
     for kr, kb in near:
         pl.semaphore_signal(barrier, inc=1, device_id=near_device(kr, kb), device_id_type=MESH)
+    pl.semaphore_signal(barrier, inc=1, device_id=twin, device_id_type=MESH)
     for ka in far:
         pl.semaphore_signal(barrier, inc=1, device_id=far_device(ka), device_id_type=MESH)
 
     def cols(h):
         return pl.ds(h * part, part)
-
-    def result_copy(l, h):
-        return pltpu.make_async_copy(
-            out.at[l, :, cols(h)], out_hbm.at[l, :, cols(h)], out_sem.at[l, h]
-        )
 
     def solve(l, h):
         residual = rhs[l, :, cols(h)].astype(F32)
         if l > 0:
-            acc = summed[h, group]
+            acc = summed[(l - 1) % 2, h, group]
             for i in range(groups - 1):
                 acc = acc + arrived[l - 1, h, i].astype(F32)
             residual = residual - acc
@@ -81,7 +78,6 @@
         out[l, :, cols(h)] = solution
         if l < last:
             gathered[l, h, side * rows + row] = solution.astype(BF16)
-        result_copy(l, h).start()
 
     def gather_copies(l, h):
         block = gathered.at[l, h, side * rows + row]
@@ -92,7 +88,24 @@
                 device_id=near_device(kr, kb), device_id_type=MESH,
             )
             for kr, kb in near
+        ] + [
+            pltpu.make_async_remote_copy(
+                src_ref=block, dst_ref=block,
+                send_sem=gsend.at[l], recv_sem=trecv.at[l, h],
+                device_id=twin, device_id_type=MESH,
+            )
         ]
+
+    def twin_copies(l, h):
+        found = []
+        for kr, kb in near:
+            block = gathered.at[l, h, ((side + kb) % pair) * rows + (row + kr) % rows]
+            found.append(pltpu.make_async_remote_copy(
+                src_ref=block, dst_ref=block,
+                send_sem=gsend.at[l], recv_sem=trecv.at[l, h],
+                device_id=twin, device_id_type=MESH,
+            ))
+        return found
 
     def scatter_copies(l, h):
         return [
@@ -111,8 +124,12 @@
         )
 
     def wait_gather(l, h):
-        ref = gathered.at[l, h, pl.ds(0, blocks - 1)]
+        ref = gathered.at[l, h, pl.ds(0, len(near))]
         bytes_of(ref, gsend.at[l], grecv.at[l, h], near_device(*near[0])).wait_recv()
+
+    def wait_twin(l, h):
+        ref = gathered.at[l, h, pl.ds(0, len(near) + 1)]
+        bytes_of(ref, gsend.at[l], trecv.at[l, h], twin).wait_recv()
 
     def wait_scatter(l, h):
         bytes_of(arrived.at[l, h], ssend.at[l], srecv.at[l, h], far_device(far[0])).wait_recv()
@@ -214,7 +231,7 @@
             total = product(0, l + 1, h, begin)
             for m in range(1, l):
                 total = total + product(m, l + 1, h, begin)
-            summed[h, pl.ds(begin, chunk)] = total
+            summed[l % 2, h, pl.ds(begin, chunk)] = total
         if l > 0:
             over_chunks(body)
 
@@ -222,8 +239,8 @@
         def body(begin):
             total = product(l, l + 1, h, begin)
             if l > 0:
-                total = total + summed[h, pl.ds(begin, chunk)]
-            summed[h, pl.ds(begin, chunk)] = total
+                total = total + summed[l % 2, h, pl.ds(begin, chunk)]
+            summed[l % 2, h, pl.ds(begin, chunk)] = total
             outgoing[l, h, pl.ds(begin, chunk)] = total.astype(BF16)
         over_chunks(body)
 
@@ -238,31 +255,41 @@
     loads[2].wait()
     loads[3].wait()
     spread_own(1)
-    pl.semaphore_wait(barrier, len(near) + len(far))
+    pl.semaphore_wait(barrier, len(near) + 1 + len(far))
     for copy in source_copies():
         copy.start()
 
+    for copy in gather_copies(0, 0):
+        copy.start()
+    for p, copy in lower_copies(1):
+        copy.start()
     for l in range(last):
         for h in range(parts):
             if l > 0:
                 wait_scatter(l - 1, h)
                 solve(l, h)
-            for copy in gather_copies(l, h):
-                copy.start()
-            if l == 0 and h == 0:
-                for p, copy in lower_copies(1):
+                for copy in gather_copies(l, h):
                     copy.start()
-        if l == 0:
-            for i, copy in enumerate(source_copies()):
-                copy.wait_recv()
-                back = pltpu.make_async_copy(far_sources.at[i], far_s.at[i], local_sem.at[5 + i])
-                back.start()
-                back.wait()
-        spread_far(l + 1)
-        for h in range(parts):
-            earlier_terms(l, h)
+                if h == 0:
+                    spread_far(l + 1)
+                    for k in range(parts):
+                        earlier_terms(l, k)
         for h in range(parts):
             wait_gather(l, h)
+            for copy in twin_copies(l, h):
+                copy.start()
+            if l == 0:
+                if h + 1 < parts:
+                    for copy in gather_copies(0, h + 1):
+                        copy.start()
+                if h == 0:
+                    for i, copy in enumerate(source_copies()):
+                        copy.wait_recv()
+                        back = pltpu.make_async_copy(far_sources.at[i], far_s.at[i], local_sem.at[5 + i])
+                        back.start()
+                        back.wait()
+                    spread_far(1)
+            wait_twin(l, h)
             newest_term(l, h)
             for copy in scatter_copies(l, h):
                 copy.start()
@@ -286,9 +313,9 @@
         wait_scatter(last - 1, h)
         solve(last, h)
     wait_sends(last - 1)
-    for l in range(levels):
-        for h in range(parts):
-            result_copy(l, h).wait()
+
+def in_hbm(x):
+    return pltpu.with_memory_space_constraint(x, pltpu.HBM)
 
 
 def on_device(rows, columns, rhs, dinv, lower, sources):
@@ -307,9 +334,8 @@
         functools.partial(kernel, rows, groups, pair, parts),
         out_shape=jax.ShapeDtypeStruct((levels, bs, width), F32),
         in_specs=[pl.BlockSpec(memory_space=pltpu.HBM)] * 4,
-        out_specs=pl.BlockSpec(memory_space=pltpu.HBM),
+        out_specs=pl.BlockSpec(memory_space=pltpu.VMEM),
         scratch_shapes=[
-            pltpu.VMEM((levels, bs, width), F32),
             pltpu.VMEM((levels, bs, width), BF16),
             pltpu.VMEM((levels, bs, bs), F32),
             pltpu.VMEM((levels, bs, 4 * bs), BF16),
@@ -319,7 +345,7 @@
             pltpu.VMEM((last, parts, pair * rows, bs, part), BF16),
             pltpu.VMEM((last, parts, groups, bs, part), BF16),
             pltpu.VMEM((last, parts, far, bs, part), BF16),
-            pltpu.VMEM((parts, groups, bs, part), F32),
+            pltpu.VMEM((2, parts, groups, bs, part), F32),
             pltpu.VMEM((pair - 1, pairs, per, columns), jnp.int32),
             pltpu.SMEM((pairs, per, columns), jnp.int32),
             pltpu.SMEM((pair - 1, pairs, per, columns), jnp.int32),
@@ -332,19 +358,19 @@
             dma((pair - 1,)),
             dma((pair - 1,)),
             dma((4 + pair,)),
-            dma((levels, parts)),
+            dma((last, parts)),
         ],
         compiler_params=pltpu.CompilerParams(
-            collective_id=0, has_side_effects=True, vmem_limit_bytes=64 * 1024 * 1024
+            collective_id=0, has_side_effects=True, vmem_limit_bytes=48*1024*1024
         ),
         cost_estimate=pl.CostEstimate(
             flops=flops, bytes_accessed=2 * lower.size, transcendentals=0
         ),
     )(
-        rhs.reshape(levels, bs, width),
-        dinv.reshape(levels, bs, bs),
-        lower.reshape(pairs, groups, pair, bs, per * bs),
-        jnp.swapaxes(sources.reshape(pairs, columns, per), 1, 2),
+        in_hbm(rhs.reshape(levels, bs, width)),
+        in_hbm(dinv.reshape(levels, bs, bs)),
+        in_hbm(lower.reshape(pairs, groups, pair, bs, per * bs)),
+        in_hbm(jnp.swapaxes(sources.reshape(pairs, columns, per), 1, 2)),
     )
     return result.reshape(levels, 1, 1, bs, width)
 

time: 36.3 us -> 38.8 us (1.069)
  Pallas kernels: 34.5 us -> 37.9 us
  local copies, waits for them, and re-layouts: 1.67 us -> 0.71 us
    pallas_call x1, Pallas kernels: 34.5 us -> 37.9 us  [on_device(): pl.pallas_call(functools.partial(kernel, rows, groups, pair, parts), out_...]
    unnamed x1, local copies, waits for them, and re-layouts: 1.67 us -> 0.71 us
where the time goes in v3:
time: 38.8 us; the launch traced here: 38.7 us
  Pallas kernels  37.9 us (98%)
  local copies, waits for them, and re-layouts  0.71 us (2%)
    pallas_call x1, Pallas kernels, on_device(): pl.pallas_call(functools.partial(kernel, rows, groups, pair, parts), out_...  37.9 us

profile of v3, /device:TPU:0, one launch (start us, length us, event | category | flops | bytes accessed | tf_op | source)
XLA Modules:
  0.0 38.7 jit_solution(15396519916723107744)
XLA Ops:
  0.0 37.9 %shard_map.46 = f32[4,64,256]{2,1,0:T(8,128)S(1)} custom-call(bf16[4,64,256]{2,1,0:T(8,128)(2,1)} %bitcast.11, f32[4,64,64]{2,1,0:T(8,128)} %bitcast.12, bf16[6,4,2,64,128]{4,3,2,1,0:T(8,128)(2,1)} %bitcast.10, s32[6,2,8]{2,1,0:T(2,128)} %bitcast.13), custom_call_target="tpu_custom_call" | custom-call | flops 402653184 | bytes 786432 | tf_op jit(solution)/shard_map/pallas_call | solution.py:333
  38.0 0.7 %copy.7 = f32[4,1,1,64,256]{4,3,2,1,0:T(8,128)} copy(f32[4,1,1,64,256]{4,3,2,1,0:T(8,128)S(1)} %bitcast.9) | data formatting | bytes 524288

commit v4 on v2

--- a/solution.py
+++ b/solution.py
@@ -18,10 +18,10 @@
 
 def kernel(
     rows, groups, pair, parts,
-    rhs_hbm, dinv_hbm, lower, sources, out_hbm,
-    out, rhs, dinv, split, mine, wide, held, gathered, outgoing, arrived, summed,
+    rhs_hbm, dinv_hbm, lower, sources, out,
+    rhs, dinv, split, mine, wide, held, gathered, outgoing, arrived, summed,
     far_sources, own_s, far_s,
-    gsend, grecv, ssend, srecv, lsend, lrecv, csend, crecv, local_sem, out_sem,
+    gsend, grecv, ssend, srecv, lsend, lrecv, csend, crecv, local_sem,
 ):
     levels, bs, width = rhs.shape
     part = width // parts
@@ -59,11 +59,6 @@
 
     def cols(h):
         return pl.ds(h * part, part)
-
-    def result_copy(l, h):
-        return pltpu.make_async_copy(
-            out.at[l, :, cols(h)], out_hbm.at[l, :, cols(h)], out_sem.at[l, h]
-        )
 
     def solve(l, h):
         residual = rhs[l, :, cols(h)].astype(F32)
@@ -81,7 +76,6 @@
         out[l, :, cols(h)] = solution
         if l < last:
             gathered[l, h, side * rows + row] = solution.astype(BF16)
-        result_copy(l, h).start()
 
     def gather_copies(l, h):
         block = gathered.at[l, h, side * rows + row]
@@ -286,9 +280,9 @@
         wait_scatter(last - 1, h)
         solve(last, h)
     wait_sends(last - 1)
-    for l in range(levels):
-        for h in range(parts):
-            result_copy(l, h).wait()
+
+def in_hbm(x):
+    return pltpu.with_memory_space_constraint(x, pltpu.HBM)
 
 
 def on_device(rows, columns, rhs, dinv, lower, sources):
@@ -307,9 +301,8 @@
         functools.partial(kernel, rows, groups, pair, parts),
         out_shape=jax.ShapeDtypeStruct((levels, bs, width), F32),
         in_specs=[pl.BlockSpec(memory_space=pltpu.HBM)] * 4,
-        out_specs=pl.BlockSpec(memory_space=pltpu.HBM),
+        out_specs=pl.BlockSpec(memory_space=pltpu.VMEM),
         scratch_shapes=[
-            pltpu.VMEM((levels, bs, width), F32),
             pltpu.VMEM((levels, bs, width), BF16),
             pltpu.VMEM((levels, bs, bs), F32),
             pltpu.VMEM((levels, bs, 4 * bs), BF16),
@@ -332,19 +325,18 @@
             dma((pair - 1,)),
             dma((pair - 1,)),
             dma((4 + pair,)),
-            dma((levels, parts)),
         ],
         compiler_params=pltpu.CompilerParams(
-            collective_id=0, has_side_effects=True, vmem_limit_bytes=64 * 1024 * 1024
+            collective_id=0, has_side_effects=True, vmem_limit_bytes=48 * 1024 * 1024
         ),
         cost_estimate=pl.CostEstimate(
             flops=flops, bytes_accessed=2 * lower.size, transcendentals=0
         ),
     )(
-        rhs.reshape(levels, bs, width),
-        dinv.reshape(levels, bs, bs),
-        lower.reshape(pairs, groups, pair, bs, per * bs),
-        jnp.swapaxes(sources.reshape(pairs, columns, per), 1, 2),
+        in_hbm(rhs.reshape(levels, bs, width)),
+        in_hbm(dinv.reshape(levels, bs, bs)),
+        in_hbm(lower.reshape(pairs, groups, pair, bs, per * bs)),
+        in_hbm(jnp.swapaxes(sources.reshape(pairs, columns, per), 1, 2)),
     )
     return result.reshape(levels, 1, 1, bs, width)
 

time: 36.3 us -> 34.7 us (0.956)
  local copies, waits for them, and re-layouts: 1.67 us -> 0.71 us
  Pallas kernels: 34.5 us -> 33.8 us
    unnamed x1, local copies, waits for them, and re-layouts: 1.67 us -> 0.71 us
    pallas_call x1, Pallas kernels: 34.5 us -> 33.8 us  [on_device(): pl.pallas_call(functools.partial(kernel, rows, groups, pair, parts), out_...]
where the time goes in v4:
time: 34.7 us; the launch traced here: 34.5 us
  Pallas kernels  33.8 us (97%)
  local copies, waits for them, and re-layouts  0.71 us (2%)
    pallas_call x1, Pallas kernels, on_device(): pl.pallas_call(functools.partial(kernel, rows, groups, pair, parts), out_...  33.8 us
    unnamed x1, local copies, waits for them, and re-layouts  0.71 us

profile of v4, /device:TPU:0, one launch (start us, length us, event | category | flops | bytes accessed | tf_op | source)
XLA Modules:
  0.0 34.5 jit_solution(6800536598121557567)
XLA Ops:
  0.0 33.8 %shard_map.46 = f32[4,64,256]{2,1,0:T(8,128)S(1)} custom-call(bf16[4,64,256]{2,1,0:T(8,128)(2,1)} %bitcast.11, f32[4,64,64]{2,1,0:T(8,128)} %bitcast.12, bf16[6,4,2,64,128]{4,3,2,1,0:T(8,128)(2,1)} %bitcast.10, s32[6,2,8]{2,1,0:T(2,128)} %bitcast.13), custom_call_target="tpu_custom_call" | custom-call | flops 402653184 | bytes 786432 | tf_op jit(solution)/shard_map/pallas_call | solution.py:300
  33.8 0.7 %copy.7 = f32[4,1,1,64,256]{4,3,2,1,0:T(8,128)} copy(f32[4,1,1,64,256]{4,3,2,1,0:T(8,128)S(1)} %bitcast.9) | data formatting | bytes 524288

commit v5 on v4

--- a/solution.py
+++ b/solution.py
@@ -290,7 +290,7 @@
     pairs = lower.shape[0]
     per = sources.shape[-1]
     pair = 2
-    parts = 2
+    parts = 1
     groups = columns // pair
     part = width // parts
     last = levels - 1

time: 34.7 us -> 35.6 us (1.026)
  Pallas kernels: 33.8 us -> 34.7 us
    pallas_call x1, Pallas kernels: 33.8 us -> 34.7 us  [on_device(): pl.pallas_call(functools.partial(kernel, rows, groups, pair, parts), out_...]
where the time goes in v5:
time: 35.6 us; the launch traced here: 35.5 us
  Pallas kernels  34.7 us (97%)
  local copies, waits for them, and re-layouts  0.71 us (2%)
    pallas_call x1, Pallas kernels, on_device(): pl.pallas_call(functools.partial(kernel, rows, groups, pair, parts), out_...  34.7 us

profile of v5, /device:TPU:0, one launch (start us, length us, event | category | flops | bytes accessed | tf_op | source)
XLA Modules:
  0.0 35.5 jit_solution(15562876263769395057)
XLA Ops:
  0.0 34.7 %shard_map.46 = f32[4,64,256]{2,1,0:T(8,128)S(1)} custom-call(bf16[4,64,256]{2,1,0:T(8,128)(2,1)} %bitcast.11, f32[4,64,64]{2,1,0:T(8,128)} %bitcast.12, bf16[6,4,2,64,128]{4,3,2,1,0:T(8,128)(2,1)} %bitcast.10, s32[6,2,8]{2,1,0:T(2,128)} %bitcast.13), custom_call_target="tpu_custom_call" | custom-call | flops 402653184 | bytes 786432 | tf_op jit(solution)/shard_map/pallas_call | solution.py:300
  34.7 0.7 %copy.7 = f32[4,1,1,64,256]{4,3,2,1,0:T(8,128)} copy(f32[4,1,1,64,256]{4,3,2,1,0:T(8,128)S(1)} %bitcast.9) | data formatting | bytes 524288
